TPU v7x, 32 devices: a whole 2x2x4 slice. The times are simulated.
32 devices in a mesh: seq: 16 (over z, x, core), head: 2 (over y).
Axes of the slice: x: 2, y: 2, z: 4, core: 2. Of those that a mesh axis runs over, the one named last changes fastest.
Arguments:
- tokens: bfloat16 [2048, 2048], P('seq'), may hold values from -17 to 17, as said below
- q_weight: bfloat16 [2048, 2048], P(None, 'head'), may hold values from -0.125 to 0.125
- k_weight: bfloat16 [2048, 256], P(None, 'head'), may hold values from -0.3125 to 0.3125
- v_weight: bfloat16 [2048, 256], P(None, 'head'), may hold values from -0.125 to 0.125
- out_weight: bfloat16 [2048, 2048], P('head'), may hold values from -1.25 to 1.25
- summary: bfloat16 [1024, 16, 2, 256], P('seq', None, None, 'head'), may hold values from -12 to 12
- links: int32 [16], P('seq'), may hold values from -1 to 1023, as said below
Outputs:
- mixed: bfloat16 [2048, 2048], P('seq', 'head')
Inputs may be any that keep to these rules, and one draw needn't show every extreme that they name: `tokens`: in the hidden draw rows have scales of their own. `links`: padding (-1) fills the tail of the list, and at least the first half of the slots are valid. Counting the valid slots by owner (id // 64), one owner has exactly 3 and none more.
All inputs are finite; a program needn't handle non-finite values.
Results may differ from a plain program's by a relative error of at most 0.01.
The roundings to bfloat16 on the way count: a program that leaves them out, or rounds other values in their place, can miss the bound.
Values may be sent and summed in bfloat16 or wider, within the bound.
A program may use at most 64 MiB of HBM per device.

v0:
```python
import math

import jax
import jax.numpy as jnp
from jax import lax
from jax.sharding import PartitionSpec as P

HEAD_DIM = 128
SUM_ROWS = 16
MOST = 3


block_keys = 1024


def shards(tokens, q_weight, k_weight, v_weight, out_weight, summary, links):
    token_count = tokens.shape[0]
    local_heads = q_weight.shape[1] // HEAD_DIM
    local_groups = k_weight.shape[1] // HEAD_DIM
    per_group = local_heads // local_groups
    scale_factor = 1.0 / math.sqrt(HEAD_DIM)
    queries = jnp.dot(tokens, q_weight, preferred_element_type=jnp.float32).astype(jnp.bfloat16)
    queries = queries.reshape(token_count, local_groups, per_group, HEAD_DIM)
    keys = jnp.dot(tokens, k_weight, preferred_element_type=jnp.float32).astype(jnp.bfloat16)
    values = jnp.dot(tokens, v_weight, preferred_element_type=jnp.float32).astype(jnp.bfloat16)

    def attend_block(state, key_rows, value_rows, allowed):
        maxima, totals, accum = state
        count = key_rows.shape[0]
        key_heads = key_rows.reshape(count, local_groups, HEAD_DIM)
        value_heads = value_rows.reshape(count, local_groups, HEAD_DIM)
        scores = (
            jnp.einsum("tkgd,nkd->tkgn", queries, key_heads, preferred_element_type=jnp.float32)
            * scale_factor
        )
        scores = jnp.where(allowed[None, None, None, :], scores, -1e30)
        new_max = jnp.maximum(maxima, jnp.max(scores, axis=3))
        factor = jnp.exp(maxima - new_max)
        weights = jnp.exp(scores - new_max[..., None])
        totals = totals * factor + jnp.sum(weights, axis=3)
        product = jnp.einsum(
            "tkgn,nkd->tkgd",
            weights.astype(jnp.bfloat16),
            value_heads,
            preferred_element_type=jnp.float32,
        )
        accum = accum * factor[..., None] + product
        return (new_max, totals, accum)

    def attend(state, key_rows, value_rows, allowed):
        count = key_rows.shape[0]
        if count > block_keys and count % block_keys == 0:
            pieces = count // block_keys

            def one_step(inner, blocks):
                return (attend_block(inner, blocks[0], blocks[1], blocks[2]), None)

            stacked = (
                key_rows.reshape(pieces, block_keys, key_rows.shape[1]),
                value_rows.reshape(pieces, block_keys, value_rows.shape[1]),
                allowed.reshape(pieces, block_keys),
            )
            state, unused = lax.scan(one_step, state, stacked)
            return state
        return attend_block(state, key_rows, value_rows, allowed)

    start_state = (
        jnp.full((token_count, local_groups, per_group), -1e30, jnp.float32),
        jnp.zeros((token_count, local_groups, per_group), jnp.float32),
        jnp.zeros((token_count, local_groups, per_group, HEAD_DIM), jnp.float32),
    )
    piece = (
        lax.all_gather(keys, "seq", axis=0, tiled=True),
        lax.all_gather(values, "seq", axis=0, tiled=True),
    )
    state = attend(start_state, piece[0], piece[1], jnp.ones((piece[0].shape[0],), bool))
    entity_count = summary.shape[0]
    every_link = lax.all_gather(links, "seq", axis=0, tiled=True)
    device_index = lax.axis_index("seq")
    owned = (every_link >= 0) & (every_link // entity_count == device_index)
    order_owned = jnp.cumsum(owned.astype(jnp.int32)) - 1
    selection = (order_owned[None, :] == jnp.arange(MOST, dtype=jnp.int32)[:, None]) & owned[
        None, :
    ]
    local_index = jnp.sum(jnp.where(selection, every_link % entity_count, 0), axis=1)
    present = jnp.any(selection, axis=1)
    owned_rows = summary[local_index]
    gathered, flags = (
        lax.all_gather(owned_rows, "seq", axis=0, tiled=True),
        lax.all_gather(present.astype(jnp.bfloat16), "seq", axis=0, tiled=True),
    )
    count = gathered.shape[0]
    key_rows = gathered[:, :, 0].reshape(count * SUM_ROWS, gathered.shape[3])
    value_rows = gathered[:, :, 1].reshape(count * SUM_ROWS, gathered.shape[3])
    allowed = jnp.repeat(flags > 0.5, SUM_ROWS)
    state = attend(state, key_rows, value_rows, allowed)
    maxima, totals, accum = state
    attended = (
        (accum / totals[..., None])
        .astype(jnp.bfloat16)
        .reshape(token_count, local_heads * HEAD_DIM)
    )
    partial_sum = jnp.dot(attended, out_weight, preferred_element_type=jnp.float32)
    return lax.psum_scatter(
        partial_sum.astype(jnp.bfloat16), "head", scatter_dimension=1, tiled=True
    )


def solution(mesh):
    placed = (
        P("seq", None),
        P(None, "head"),
        P(None, "head"),
        P(None, "head"),
        P("head", None),
        P("seq", None, None, "head"),
        P("seq"),
    )
    return jax.shard_map(
        shards, mesh=mesh, in_specs=placed, out_specs=P("seq", "head"), check_vma=False
    )
```

profile of v0, /device:TPU:0, one launch (start us, length us, event | category | flops | bytes accessed | tf_op | source)
XLA Modules:
  0.0 149.3 jit_solution(14080646145605821692)
XLA Ops:
  6.5 0.0 copy-start
  6.5 0.0 reduce-scatter.2.cloned.1.call-start
  7.3 1.2 dynamic-slice
  8.5 0.8 dynamic-update-slice
  9.9 13.7 %all-reduce = s32[16]{0:T(128)S(1)} all-reduce(s32[16]{0:T(128)S(1)} %dynamic-update-slice), channel_id=1, replica_groups=mesh['seq'=16,'head'=2] {'seq'}, use_global_device_ids=true, to_apply=%add | all-reduce | flops 16 | bytes 128
  23.7 0.1 copy.42
  23.8 0.1 add_reduce_fusion
  23.9 0.1 fusion.50
  24.0 0.1 select_reduce_fusion
  24.2 0.2 dynamic-update-slice.1
  24.4 29.5 %all-reduce.1 = bf16[48]{0:T(256)(128)(2,1)S(1)} all-reduce(bf16[48]{0:T(256)(128)(2,1)S(1)} %dynamic-update-slice.1), channel_id=1, replica_groups=mesh['seq'=16,'head'=2] {'seq'}, use_global_device_ids=true, to_apply=%add.1 | all-reduce | flops 48 | bytes 192
  53.9 0.1 broadcast_in_dim.55
  54.0 0.1 broadcast_in_dim.56
  54.1 1.7 %gather_fusion = bf16[3,16,2,128]{3,2,1,0:T(2,128)(2,1)S(1)} fusion(bf16[64,16,2,128]{3,2,1,0:T(2,128)(2,1)} %param.14, s32[1024]{0:T(1024)S(1)} %pad_clamp_fusion), kind=kCustom, calls=%fused_computation | custom fusion | bytes 49164 | tf_op jit(solution)/shard_map/gather | solution.py:87
  55.8 0.0 copy-done
  55.8 1.3 convolution_convert_fusion.3
  57.1 1.3 convolution_convert_fusion.2
  58.4 2.9 %convolution_convert_fusion.1 = bf16[128,1024]{1,0:T(8,128)(2,1)S(1)} fusion(bf16[128,2048]{1,0:T(8,128)(2,1)S(1)} %copy-done, bf16[2048,1024]{1,0:T(8,128)(2,1)} %param.10), kind=kOutput, calls=%fused_computation.39 | convolution fusion | flops 537001984 | bytes 4980736 | tf_op jit(solution)/shard_map/dot_general | solution.py:22
  61.4 18.3 %all-gather = bf16[48,16,2,128]{3,1,2,0:T(8,128)(2,1)S(1)} all-gather(bf16[3,16,2,128]{3,1,2,0:T(8,128)(2,1)S(1)} %copy.43), channel_id=2, replica_groups=mesh['seq'=16,'head'=2] {'seq'}, dimensions={0}, use_global_device_ids=true | all-gather | bytes 417792 | tf_op jit(solution)/shard_map/all_gather | solution.py:89
  79.7 20.7 %all_gather.16 = bf16[2048,128]{1,0:T(8,128)(2,1)S(1)} all-gather(bf16[128,128]{1,0:T(8,128)(2,1)S(1)} %convolution_convert_fusion.2), channel_id=1, replica_groups=mesh['seq'=16,'head'=2] {'seq'}, dimensions={0}, use_global_device_ids=true | all-gather | bytes 557056 | tf_op jit(solution)/shard_map/all_gather | solution.py:74
  100.5 18.9 %all_gather.15 = bf16[2048,128]{1,0:T(8,128)(2,1)S(1)} all-gather(bf16[128,128]{1,0:T(8,128)(2,1)S(1)} %convolution_convert_fusion.3), channel_id=1, replica_groups=mesh['seq'=16,'head'=2] {'seq'}, dimensions={0}, use_global_device_ids=true | all-gather | bytes 557056 | tf_op jit(solution)/shard_map/all_gather | solution.py:73
  119.3 4.9 %while.15 = (s32[]{:T(128)}, f32[128,1,8]{0,2,1:T(8,128)S(1)}, f32[128,1,8]{0,2,1:T(8,128)S(1)}, f32[128,1,8,128]{0,3,2,1:T(8,128)S(1)}, bf16[2,1024,128]{2,1,0:...) while((s32[]{:T(128)}, f32[128,1,8]{0,2,1:T(8,128)S(1)}, ...), condition=%wide.region_3.4_spmd.clone, body=%wide.region_0.3_spmd.clone.sunk | while | flops 545658880 | bytes 14483577 | solution.py:63
  119.3 0.7 bitcast_reduce_fusion.3
  120.1 0.7 fusion.74
  120.8 1.0 fusion.75
  121.8 0.7 bitcast_reduce_fusion.3
  122.5 0.7 fusion.74
  123.2 1.0 fusion.75
  124.2 0.6 bitcast_reduce_fusion.1
  124.9 0.7 fusion.25
  125.6 0.0 copy-start.1
  125.6 1.0 fusion.40
  126.6 1.2 copy-done.1
  127.8 1.5 %convolution_convert_fusion = bf16[128,2048]{1,0:T(8,128)(2,1)} fusion(bf16[128,1024]{0,1:T(8,128)(2,1)S(1)} %bitcast.210, bf16[1024,2048]{1,0:T(8,128)(2,1)S(1)} %copy-done.1), kind=kOutput, calls=%fused_computation.31 | convolution fusion | flops 537133056 | bytes 4980736 | tf_op jit(solution)/shard_map/dot_general | solution.py:103
  129.3 0.0 reduce-scatter.2.cloned.1.call-update
  129.3 13.2 %reduce-scatter.2.cloned.1.call-done = bf16[128,1024]{1,0:T(8,128)(2,1)} async-done(((bf16[128,2048]{1,0:T(8,128)(2,1)}), bf16[128,1024]{1,0:T(8,128)(2,1)}) %reduce-scatter.2.cloned.1.call-update) | async-done | bytes 262160 | tf_op jit(solution)/shard_map/reduce_scatter | solution.py:104
  (24 shorter events, 0.3 us)
Async XLA Ops:
  6.5 49.2 %copy-start = (bf16[128,2048]{1,0:T(8,128)(2,1)S(1)}, bf16[128,2048]{1,0:T(8,128)(2,1)}, u32[]{:S(2)}) copy-start(bf16[128,2048]{1,0:T(8,128)(2,1)} %param.9) | copy-start | bytes 1572868
  6.5 136.0 %reduce-scatter.2.cloned.1.call-start = ((), (), s32[]{:S(2)}) async-start(), calls=%async_computation.1 | async-start | bytes 786432 | tf_op jit(solution)/shard_map/reduce_scatter | solution.py:104
  125.6 2.2 %copy-start.1 = (bf16[1024,2048]{1,0:T(8,128)(2,1)S(1)}, bf16[1024,2048]{1,0:T(8,128)(2,1)}, u32[]{:S(2)}) copy-start(bf16[1024,2048]{1,0:T(8,128)(2,1)} %param.13) | copy-start | bytes 12582916
Sparse Core Ops, SparseCore 0:
  129.4 13.0 reduce-scatter.1
where the time goes:
time: 150 us; the launch traced here: 149 us
  blocking collectives  101 us (67%)
  between operations  14.9 us (10%)
  waiting for transfers between devices  13.2 us (9%)
  matrix products  12 us (8%)
  local copies, waits for them, and re-layouts  5.46 us (4%)
  other arithmetic  2.59 us (2%)
    unnamed x2, blocking collectives  43.2 us
    all_gather x1, blocking collectives, shards(): lax.all_gather(values, 'seq', axis=0, tiled=True)  20.7 us
    all_gather x1, blocking collectives, shards(): lax.all_gather(keys, 'seq', axis=0, tiled=True)  18.9 us
    all_gather x1, blocking collectives, shards(): lax.all_gather(owned_rows, 'seq', axis=0, tiled=True)  18.3 us
    reduce_scatter x1, waiting for transfers between devices, shards(): lax.psum_scatter(partial_sum.astype(jnp.bfloat16), 'head', scatter_dimens...  13.2 us
    unnamed x11, local copies, waits for them, and re-layouts  3.52 us
  transfers between devices with their start and end apart: 1, of which 1 were waited for; matrix products, arithmetic and copies ran while one was open for 0% of the time, Pallas kernels for 0%

commit v1 on v0

v1 whole, which is shorter than its diff:
```python
import functools
import math

import jax
import jax.numpy as jnp
from jax import lax
from jax.experimental import pallas as pl
from jax.experimental.pallas import tpu as pltpu
from jax.sharding import PartitionSpec as P

HEAD_DIM = 128
SUM_ROWS = 16
MOST = 3
MESH = pl.DeviceIdType.MESH
F32 = jnp.float32
BF16 = jnp.bfloat16


def each(low, high, step):
    if high - low <= 8:
        for i in range(low, high):
            step(i)
    else:
        lax.fori_loop(low, high, lambda i, carry: (step(i), carry)[1], 0)


def kernel(
    n, entities, link_dev,
    tok_hbm, qw_hbm, kw_hbm, vw_hbm, ow_hbm, sum_hbm, links_ref,
    out_ref,
    tok, qw, kvw, ow, summ, q, kv, rows, link_v, link_s, att, part, y_send, y_recv,
    load_sem, kv_recv, row_recv, link_recv, link_send,
    kv_send_a, kv_send_b, kv_send_c, row_send_a, row_send_b, row_send_c,
    y_send_sem, y_recv_sem,
):
    me = lax.axis_index("seq")
    hd = lax.axis_index("head")
    size = n // 4
    a, b, c = me // 4, (me // 2) % 2, me % 2
    slots = n * link_dev
    t = tok.shape[0]
    heads = q.shape[0] // t

    def ident(a_, b_, c_):
        return (a_ * 2 + b_) * 2 + c_

    loads = [
        pltpu.make_async_copy(tok_hbm, tok, load_sem.at[0]),
        pltpu.make_async_copy(kw_hbm, kvw.at[:, pl.ds(0, HEAD_DIM)], load_sem.at[1]),
        pltpu.make_async_copy(vw_hbm, kvw.at[:, pl.ds(HEAD_DIM, HEAD_DIM)], load_sem.at[2]),
        pltpu.make_async_copy(sum_hbm, summ, load_sem.at[3]),
        pltpu.make_async_copy(qw_hbm, qw, load_sem.at[4]),
        pltpu.make_async_copy(ow_hbm, ow, load_sem.at[5]),
    ]
    for item in loads:
        item.start()

    barrier = pltpu.get_barrier_semaphore()

    def greet(k):
        pl.semaphore_signal(
            barrier, inc=1, device_id=(lax.rem(me + k, n), hd), device_id_type=MESH
        )

    each(1, n, greet)
    pl.semaphore_signal(barrier, inc=1, device_id=(me, 1 - hd), device_id_type=MESH)

    lane = lax.broadcasted_iota(jnp.int32, (1, 128), 1)
    mine = jnp.full((1, 128), -1, jnp.int32)
    for i in range(link_dev):
        mine = jnp.where(lane == i, links_ref[i], mine)
    link_v[me] = mine

    pl.semaphore_wait(barrier, n)

    def link_copy(k, src):
        return pltpu.make_async_remote_copy(
            src_ref=link_v.at[src], dst_ref=link_v.at[src],
            send_sem=link_send.at[k], recv_sem=link_recv.at[src],
            device_id=(lax.rem(me + k, n), hd), device_id_type=MESH,
        )

    each(1, n, lambda k: link_copy(k, me).start())

    for i in range(3):
        loads[i].wait()
    kv_mine = jnp.dot(tok[...], kvw[...], preferred_element_type=F32).astype(BF16)
    kv[pl.ds(pl.multiple_of(me * t, t), t), :] = kv_mine

    def kv_block(src):
        return kv.at[pl.ds(pl.multiple_of(src * t, t), t), :]

    def kv_copy(src, target, send):
        return pltpu.make_async_remote_copy(
            src_ref=kv_block(src), dst_ref=kv_block(src),
            send_sem=send, recv_sem=kv_recv.at[src],
            device_id=(target, hd), device_id_type=MESH,
        )

    def row_copy(src, target, send):
        return pltpu.make_async_remote_copy(
            src_ref=rows.at[src], dst_ref=rows.at[src],
            send_sem=send, recv_sem=row_recv.at[src],
            device_id=(target, hd), device_id_type=MESH,
        )

    kv_set = (kv_copy, kv_send_a, kv_send_b, kv_send_c)
    row_set = (row_copy, row_send_a, row_send_b, row_send_c)

    def across(copy_of, send_a, send_b, send_c, k):
        return copy_of(me, ident(lax.rem(a + k, size), b, c), send_a.at[k])

    def to_b(copy_of, send_a, send_b, send_c, a_):
        return copy_of(ident(a_, b, c), ident(a, 1 - b, c), send_b.at[a_])

    def to_c(copy_of, send_a, send_b, send_c, a_, b_):
        return copy_of(ident(a_, b_, c), ident(a, b, 1 - c), send_c.at[a_ * 2 + b_])

    def first(group):
        each(1, size, lambda k: across(*group, k).start())
        to_b(*group, a).start()
        to_c(*group, a, b).start()

    def got(group, src):
        group[0](src, me, group[1].at[0]).wait_recv()

    def relay_a(group):
        def one(k):
            a_ = lax.rem(a + k, size)
            got(group, ident(a_, b, c))
            to_b(*group, a_).start()
            to_c(*group, a_, b).start()

        each(1, size, one)

    def relay_b(group):
        def one(k):
            a_ = lax.rem(a + k, size)
            got(group, ident(a_, 1 - b, c))
            to_c(*group, a_, 1 - b).start()

        each(0, size, one)

    def finish(group):
        def one(k):
            got(group, ident(k // 2, k % 2, 1 - c))

        each(0, 2 * size, one)

    def sent(group):
        each(1, size, lambda k: across(*group, k).wait_send())
        each(0, size, lambda k: to_b(*group, k).wait_send())
        each(0, 2 * size, lambda k: to_c(*group, k // 2, k % 2).wait_send())

    first(kv_set)

    each(1, n, lambda k: link_copy(k, lax.rem(me + k, n)).wait_recv())
    to_scalar = pltpu.make_async_copy(link_v, link_s, load_sem.at[6])
    to_scalar.start()
    to_scalar.wait()
    loads[3].wait()

    def link_at(s):
        return link_s[s // link_dev, 0, s % link_dev]

    def pick(s, carry):
        count, valid, chosen = carry
        v = link_at(s)
        safe = jnp.maximum(v, 0)
        own = jnp.where((v >= 0) & (lax.div(safe, entities) == me), 1, 0)
        local = lax.rem(safe, entities)
        chosen = tuple(
            jnp.where((own == 1) & (count == j), local, chosen[j]) for j in range(MOST)
        )
        return (count + own, valid + jnp.where(v >= 0, 1, 0), chosen)

    carry = (jnp.int32(0), jnp.int32(0), (jnp.int32(0),) * MOST)
    if slots <= 16:
        for s in range(slots):
            carry = pick(s, carry)
    else:
        carry = lax.fori_loop(0, slots, pick, carry)
    unused, valid_count, chosen = carry
    half = MOST * SUM_ROWS
    raw = jnp.concatenate([summ[chosen[j]] for j in range(MOST)], axis=0)
    r_out = lax.broadcasted_iota(jnp.int32, (2 * half, 2 * half), 0)
    r_in = lax.broadcasted_iota(jnp.int32, (2 * half, 2 * half), 1)
    perm = jnp.where(
        r_in == jnp.where(r_out < half, 2 * r_out, 2 * (r_out - half) + 1), 1.0, 0.0
    ).astype(BF16)
    split = jnp.dot(perm, raw, preferred_element_type=F32).astype(BF16)
    for j in range(2 * MOST):
        rows[me, j] = split[j * SUM_ROWS:(j + 1) * SUM_ROWS]
    first(row_set)

    loads[4].wait()

    def project(p):
        result = jnp.dot(
            tok[...], qw[:, p * 256:(p + 1) * 256], preferred_element_type=F32
        ).astype(BF16)
        for i in range(2):
            q[(2 * p + i) * t:(2 * p + i + 1) * t, :] = result[:, i * 128:(i + 1) * 128]

    pairs = heads // 2
    project(0)
    project(1)
    relay_a(kv_set)
    for p in range(2, pairs):
        project(p)
    relay_b(kv_set)
    relay_a(row_set)
    relay_b(row_set)
    finish(kv_set)
    finish(row_set)

    def place(s):
        v = link_at(s)
        safe = jnp.maximum(v, 0)
        owner = lax.div(safe, entities)

        def same(s2, total):
            w = link_at(s2)
            return total + jnp.where((w >= 0) & (lax.div(jnp.maximum(w, 0), entities) == owner), 1, 0)

        rank = jnp.int32(0)
        if slots <= 16:
            for s2 in range(s):
                rank = same(s2, rank)
        else:
            rank = lax.fori_loop(0, s, same, rank)
        rank = jnp.where(v >= 0, jnp.minimum(rank, MOST - 1), 0)
        start = n * t + s * SUM_ROWS
        if not isinstance(s, int):
            start = pl.multiple_of(start, SUM_ROWS)
        kv[pl.ds(start, SUM_ROWS), pl.ds(0, HEAD_DIM)] = rows[owner, rank]
        kv[pl.ds(start, SUM_ROWS), pl.ds(HEAD_DIM, HEAD_DIM)] = rows[owner, MOST + rank]

    if slots <= 16:
        for s in range(slots):
            place(s)
    else:
        lax.fori_loop(0, slots, lambda s, carry: (place(s), carry)[1], 0)

    factor = math.log2(math.e) / math.sqrt(HEAD_DIM)
    total_keys = kv.shape[0]
    chunk = 16 * t + 256
    if total_keys % chunk:
        chunk = t
    limit = n * t + valid_count * SUM_ROWS

    def attend(p, unused_carry):
        queries = q[pl.ds(pl.multiple_of(p * 2 * t, 2 * t), 2 * t), :]

        def one_chunk(i, state):
            top, total, accum = state
            start = i * chunk
            if not isinstance(i, int):
                start = pl.multiple_of(start, chunk)
            scores = lax.dot_general(
                queries, kv[pl.ds(start, chunk), pl.ds(0, HEAD_DIM)],
                (((1,), (1,)), ((), ())), preferred_element_type=F32,
            )
            column = lax.broadcasted_iota(jnp.int32, (1, chunk), 1) + start
            scores = jnp.where(column < limit, scores, -1e30)
            new_top = jnp.maximum(top, jnp.max(scores, axis=1, keepdims=True))
            change = jnp.exp2((top - new_top) * factor)
            weights = jnp.exp2((scores - new_top) * factor)
            total = total * change + jnp.sum(weights, axis=1, keepdims=True)
            product = jnp.dot(
                weights.astype(BF16), kv[pl.ds(start, chunk), pl.ds(HEAD_DIM, HEAD_DIM)],
                preferred_element_type=F32,
            )
            return (new_top, total, accum * change + product)

        state = (
            jnp.full((2 * t, 1), -1e30, F32),
            jnp.zeros((2 * t, 1), F32),
            jnp.zeros((2 * t, HEAD_DIM), F32),
        )
        if total_keys == chunk:
            state = one_chunk(0, state)
        else:
            state = lax.fori_loop(0, total_keys // chunk, one_chunk, state)
        result = (state[2] / state[1]).astype(BF16)
        att[2 * p] = result[:t]
        att[2 * p + 1] = result[t:]
        return unused_carry

    lax.fori_loop(0, pairs, attend, 0)

    loads[5].wait()
    attended = jnp.concatenate([att[h] for h in range(heads)], axis=1)
    width = out_ref.shape[1]
    pieces = y_send.shape[0]
    piece = width // pieces

    def y_copy(i):
        return pltpu.make_async_remote_copy(
            src_ref=y_send.at[i], dst_ref=y_recv.at[i],
            send_sem=y_send_sem.at[i], recv_sem=y_recv_sem.at[i],
            device_id=(me, 1 - hd), device_id_type=MESH,
        )

    def out_piece(side, i):
        start = pl.multiple_of(side * width + i * piece, piece)
        return jnp.dot(attended, ow[:, pl.ds(start, piece)], preferred_element_type=F32)

    for i in range(pieces):
        y_send[i] = out_piece(1 - hd, i).astype(BF16)
        y_copy(i).start()
    for i in range(pieces):
        part[:, i * piece:(i + 1) * piece] = out_piece(hd, i)
    for i in range(pieces):
        y_copy(i).wait_recv()
        out_ref[:, i * piece:(i + 1) * piece] = (
            part[:, i * piece:(i + 1) * piece] + y_recv[i].astype(F32)
        ).astype(BF16)
    for i in range(pieces):
        y_copy(i).wait_send()
    each(1, n, lambda k: link_copy(k, me).wait_send())
    sent(kv_set)
    sent(row_set)


def shards(n, tokens, q_weight, k_weight, v_weight, out_weight, summary, links):
    t, d = tokens.shape
    local = q_weight.shape[1]
    heads = local // HEAD_DIM
    width = out_weight.shape[1] // 2
    entities = summary.shape[0]
    link_dev = links.shape[0]
    pieces = 4
    size = n // 4
    flat = summary.reshape(entities, SUM_ROWS * 2, HEAD_DIM)
    dma = pltpu.SemaphoreType.DMA
    hbm = pl.BlockSpec(memory_space=pl.ANY)
    return pl.pallas_call(
        functools.partial(kernel, n, entities, link_dev),
        out_shape=jax.ShapeDtypeStruct((t, width), BF16),
        in_specs=[hbm] * 6 + [pl.BlockSpec(memory_space=pltpu.SMEM)],
        out_specs=pl.BlockSpec(memory_space=pltpu.VMEM),
        scratch_shapes=[
            pltpu.VMEM((t, d), BF16),
            pltpu.VMEM((d, local), BF16),
            pltpu.VMEM((d, 2 * HEAD_DIM), BF16),
            pltpu.VMEM(out_weight.shape, BF16),
            pltpu.VMEM(flat.shape, BF16),
            pltpu.VMEM((heads * t, HEAD_DIM), BF16),
            pltpu.VMEM((n * t + n * link_dev * SUM_ROWS, 2 * HEAD_DIM), BF16),
            pltpu.VMEM((n, 2 * MOST, SUM_ROWS, HEAD_DIM), BF16),
            pltpu.VMEM((n, 1, 128), jnp.int32),
            pltpu.SMEM((n, 1, 128), jnp.int32),
            pltpu.VMEM((heads, t, HEAD_DIM), BF16),
            pltpu.VMEM((t, width), F32),
            pltpu.VMEM((pieces, t, width // pieces), BF16),
            pltpu.VMEM((pieces, t, width // pieces), BF16),
            dma((7,)), dma((n,)), dma((n,)), dma((n,)), dma((n,)),
            dma((size,)), dma((size,)), dma((2 * size,)),
            dma((size,)), dma((size,)), dma((2 * size,)),
            dma((pieces,)), dma((pieces,)),
        ],
        compiler_params=pltpu.CompilerParams(
            collective_id=0, has_side_effects=True, vmem_limit_bytes=56 * 1024 * 1024
        ),
    )(tokens, q_weight, k_weight, v_weight, out_weight, flat, links)


def solution(mesh):
    placed = (
        P("seq", None),
        P(None, "head"),
        P(None, "head"),
        P(None, "head"),
        P("head", None),
        P("seq", None, None, "head"),
        P("seq"),
    )
    return jax.shard_map(
        functools.partial(shards, mesh.shape["seq"]),
        mesh=mesh, in_specs=placed, out_specs=P("seq", "head"), check_vma=False,
    )
```

time: 150 us -> 41.1 us (0.27)
  the two profiles are of different devices: /device:TPU:0 before, /device:TPU:9 now
where the time goes in v1:
time: 41.1 us; the launch traced here: 41 us
  Pallas kernels  38.6 us (94%)
  local copies, waits for them, and re-layouts  1.67 us (4%)
  between operations  0.66 us (2%)
    pallas_call x1, Pallas kernels, shards(): pl.pallas_call(functools.partial(kernel, n, entities, link_dev), out_shap...  38.6 us
    unnamed x1, local copies, waits for them, and re-layouts  1.67 us

profile of v1, /device:TPU:9, one launch (start us, length us, event | category | flops | bytes accessed | tf_op | source)
XLA Modules:
  0.0 41.0 jit_solution(17368037589924922551)
XLA Ops:
  0.7 38.6 %shard_map.73 = bf16[128,1024]{1,0:T(8,128)(2,1)} custom-call(bf16[128,2048]{1,0:T(8,128)(2,1)} %tok_hbm.1, bf16[2048,1024]{1,0:T(8,128)(2,1)} %qw_hbm.1, bf16[2048,128]{1,0:T(8,128)(2,1)} %kw_hbm.1, bf16[2048,128]{1,0:T(8,128)(2,1)} %vw_hbm.1, bf16[1024,2048]{1,0:T(8,128)(2,1)} %ow_hbm.1, bf16[64,32,128]{2,1,0:T(8,128)(2,1)} %bitcast.1, s32[1]{0:T(128)S(6)} %copy.9.links_ref), custom_call_target="tpu_custom_call" | custom-call | tf_op jit(solution)/shard_map/pallas_call | solution.py:338
  39.3 1.7 %copy.10 = bf16[128,1024]{1,0:T(8,128)(2,1)} copy(bf16[128,1024]{1,0:T(8,128)(2,1)} %shard_map.73) | data formatting | bytes 524288

commit v2 on v1

v2 whole, which is shorter than its diff:
```python
import functools
import math

import jax
import jax.numpy as jnp
from jax import lax
from jax.experimental import pallas as pl
from jax.experimental.pallas import tpu as pltpu
from jax.sharding import PartitionSpec as P

HEAD_DIM = 128
SUM_ROWS = 16
MOST = 3
MESH = pl.DeviceIdType.MESH
F32 = jnp.float32
BF16 = jnp.bfloat16


def each(low, high, step):
    if high - low <= 8:
        for i in range(low, high):
            step(i)
    else:
        lax.fori_loop(low, high, lambda i, carry: (step(i), carry)[1], 0)


def kernel(
    n, entities, link_dev,
    tok_hbm, qw_hbm, kw_hbm, vw_hbm, ow_hbm, sum_hbm, links_ref,
    out_ref,
    tok, qw, kvw, ow, summ, q, kv, rows, link_v, link_s, att, part, y_send, y_recv,
    top_ref, sum_ref, acc_ref,
    load_sem, kv_recv, row_recv, link_recv, link_send, link_recv_bc, link_send_bc,
    kv_send_a, kv_send_b, kv_send_c, row_send_a, row_send_b, row_send_c,
    y_send_sem, y_recv_sem,
):
    me = lax.axis_index("seq")
    hd = lax.axis_index("head")
    size = n // 4
    a, b, c = me // 4, (me // 2) % 2, me % 2
    slots = n * link_dev
    t = tok.shape[0]
    ht = t // 2
    heads = q.shape[0] // t
    block = heads * ht // 2
    part_keys = size * t

    def ident(a_, b_, c_):
        return (a_ * 2 + b_) * 2 + c_

    def place_of(a_, b_, c_):
        return (c_ * 2 + b_) * size + a_

    mine_at = place_of(a, b, c)

    def other(k):
        if size != 4:
            return lax.rem(a + k, size)
        end = 1 - ((a + 1) // 2) % 2
        if k == 1:
            return a + 1 - 2 * (a % 2)
        two, three = lax.rem(a + 2, 4), 3 - a
        return two * end + three * (1 - end) if k == 2 else three * end + two * (1 - end)

    loads = [
        pltpu.make_async_copy(tok_hbm, tok, load_sem.at[0]),
        pltpu.make_async_copy(kw_hbm, kvw.at[:, pl.ds(0, HEAD_DIM)], load_sem.at[1]),
        pltpu.make_async_copy(vw_hbm, kvw.at[:, pl.ds(HEAD_DIM, HEAD_DIM)], load_sem.at[2]),
        pltpu.make_async_copy(sum_hbm, summ, load_sem.at[3]),
        pltpu.make_async_copy(qw_hbm, qw, load_sem.at[4]),
        pltpu.make_async_copy(ow_hbm, ow, load_sem.at[5]),
    ]

    barrier = pltpu.get_barrier_semaphore()

    def greet(target, head):
        pl.semaphore_signal(barrier, inc=1, device_id=(target, head), device_id_type=MESH)

    each(1, size, lambda k: greet(ident(lax.rem(a + k, size), b, c), hd))
    greet(ident(a, 1 - b, c), hd)
    greet(ident(a, b, 1 - c), hd)
    greet(me, 1 - hd)
    for item in loads:
        item.start()

    lane = lax.broadcasted_iota(jnp.int32, (1, 128), 1)
    mine = jnp.full((1, 128), -1, jnp.int32)
    for i in range(link_dev):
        mine = jnp.where(lane == i, links_ref[i], mine)
    link_v[mine_at] = mine
    top_ref[...] = jnp.full(top_ref.shape, -1e30, F32)
    sum_ref[...] = jnp.zeros(sum_ref.shape, F32)
    acc_ref[...] = jnp.zeros(acc_ref.shape, F32)

    pl.semaphore_wait(barrier, size + 2)

    def link_a(src_a, target_a):
        at = place_of(src_a, b, c)
        return pltpu.make_async_remote_copy(
            src_ref=link_v.at[at], dst_ref=link_v.at[at],
            send_sem=link_send.at[target_a], recv_sem=link_recv.at[src_a],
            device_id=(ident(target_a, b, c), hd), device_id_type=MESH,
        )

    def link_b(b_, target_b):
        part_of = link_v.at[pl.ds((c * 2 + b_) * size, size)]
        return pltpu.make_async_remote_copy(
            src_ref=part_of, dst_ref=part_of,
            send_sem=link_send_bc.at[0], recv_sem=link_recv_bc.at[0],
            device_id=(ident(a, target_b, c), hd), device_id_type=MESH,
        )

    def link_c(c_, target_c):
        part_of = link_v.at[pl.ds(c_ * 2 * size, 2 * size)]
        return pltpu.make_async_remote_copy(
            src_ref=part_of, dst_ref=part_of,
            send_sem=link_send_bc.at[1], recv_sem=link_recv_bc.at[1],
            device_id=(ident(a, b, target_c), hd), device_id_type=MESH,
        )

    each(1, size, lambda k: link_a(a, lax.rem(a + k, size)).start())

    for i in range(3):
        loads[i].wait()
    kv_mine = jnp.dot(tok[...], kvw[...], preferred_element_type=F32).astype(BF16)
    kv[pl.ds(pl.multiple_of(mine_at * t, t), t), :] = kv_mine

    def kv_copy(src, target, send):
        held = kv.at[pl.ds(pl.multiple_of(src * t, t), t), :]
        return pltpu.make_async_remote_copy(
            src_ref=held, dst_ref=held,
            send_sem=send, recv_sem=kv_recv.at[src],
            device_id=(target, hd), device_id_type=MESH,
        )

    def row_copy(src, target, send):
        return pltpu.make_async_remote_copy(
            src_ref=rows.at[src], dst_ref=rows.at[src],
            send_sem=send, recv_sem=row_recv.at[src],
            device_id=(target, hd), device_id_type=MESH,
        )

    kv_set = (kv_copy, kv_send_a, kv_send_b, kv_send_c)
    row_set = (row_copy, row_send_a, row_send_b, row_send_c)

    def across(copy_of, send_a, send_b, send_c, k):
        a_ = other(k)
        return copy_of(mine_at, ident(a_, b, c), send_a.at[a_])

    def to_b(copy_of, send_a, send_b, send_c, a_):
        return copy_of(place_of(a_, b, c), ident(a, 1 - b, c), send_b.at[a_])

    def to_c(copy_of, send_a, send_b, send_c, a_, b_):
        return copy_of(place_of(a_, b_, c), ident(a, b, 1 - c), send_c.at[a_ * 2 + b_])

    def first(group):
        each(1, size, lambda k: across(*group, k).start())
        to_b(*group, a).start()
        to_c(*group, a, b).start()

    def got(group, src):
        group[0](src, me, group[1].at[0]).wait_recv()

    def relay_a(group):
        def one(k):
            a_ = other(k)
            got(group, place_of(a_, b, c))
            to_b(*group, a_).start()
            to_c(*group, a_, b).start()

        each(1, size, one)

    def relay_b(group):
        def one(k):
            a_ = a if isinstance(k, int) and k == 0 else other(k)
            got(group, place_of(a_, 1 - b, c))
            to_c(*group, a_, 1 - b).start()

        each(0, size, one)

    def finish(group, b_):
        each(0, size, lambda a_: got(group, place_of(a_, b_, 1 - c)))

    def sent(group):
        each(1, size, lambda k: across(*group, k).wait_send())
        each(0, size, lambda k: to_b(*group, k).wait_send())
        each(0, 2 * size, lambda k: to_c(*group, k // 2, k % 2).wait_send())

    first(kv_set)

    def project(p):
        result = jnp.dot(
            tok[...], qw[:, p * 256:(p + 1) * 256], preferred_element_type=F32
        ).astype(BF16)
        for i in range(2):
            for side in range(2):
                start = (side * heads + 2 * p + i) * ht
                q[start:start + ht, :] = result[side * ht:(side + 1) * ht, i * 128:(i + 1) * 128]

    pairs = heads // 2
    each(1, size, lambda k: link_a(lax.rem(a + k, size), a).wait_recv())
    link_b(b, 1 - b).start()
    loads[4].wait()
    project(0)
    link_b(1 - b, b).wait_recv()
    link_c(c, 1 - c).start()
    project(1)
    link_c(1 - c, c).wait_recv()
    to_scalar = pltpu.make_async_copy(link_v, link_s, load_sem.at[6])
    to_scalar.start()
    to_scalar.wait()
    loads[3].wait()

    def link_at(s):
        seat = s // link_dev
        return link_s[place_of(seat // 4, (seat // 2) % 2, seat % 2), 0, s % link_dev]

    def pick(s, carry):
        count, valid, chosen = carry
        v = link_at(s)
        safe = jnp.maximum(v, 0)
        own = jnp.where((v >= 0) & (lax.div(safe, entities) == me), 1, 0)
        local = lax.rem(safe, entities)
        chosen = tuple(
            jnp.where((own == 1) & (count == j), local, chosen[j]) for j in range(MOST)
        )
        return (count + own, valid + jnp.where(v >= 0, 1, 0), chosen)

    carry = (jnp.int32(0), jnp.int32(0), (jnp.int32(0),) * MOST)
    if slots <= 16:
        for s in range(slots):
            carry = pick(s, carry)
    else:
        carry = lax.fori_loop(0, slots, pick, carry)
    unused, valid_count, chosen = carry
    half = MOST * SUM_ROWS
    raw = jnp.concatenate([summ[chosen[j]] for j in range(MOST)], axis=0)
    r_out = lax.broadcasted_iota(jnp.int32, (2 * half, 2 * half), 0)
    r_in = lax.broadcasted_iota(jnp.int32, (2 * half, 2 * half), 1)
    perm = jnp.where(
        r_in == jnp.where(r_out < half, 2 * r_out, 2 * (r_out - half) + 1), 1.0, 0.0
    ).astype(BF16)
    split = jnp.dot(perm, raw, preferred_element_type=F32).astype(BF16)
    for j in range(2 * MOST):
        rows[mine_at, j] = split[j * SUM_ROWS:(j + 1) * SUM_ROWS]
    first(row_set)

    factor = math.log2(math.e) / math.sqrt(HEAD_DIM)
    limit = n * t + valid_count * SUM_ROWS

    def one_step(r0, start, count, masked):
        here = pl.ds(r0, block)
        scores = lax.dot_general(
            q[here, :], kv[pl.ds(start, count), pl.ds(0, HEAD_DIM)],
            (((1,), (1,)), ((), ())), preferred_element_type=F32,
        )
        if masked:
            column = lax.broadcasted_iota(jnp.int32, (1, count), 1) + start
            scores = jnp.where(column < limit, scores, -1e30)
        groups = [scores[:, g * 128:(g + 1) * 128] for g in range(count // 128)]
        old = top_ref[here, :]
        high = functools.reduce(jnp.maximum, groups)
        new = jnp.maximum(old, jnp.max(high, axis=1, keepdims=True))
        change = jnp.exp2((old - new) * factor)
        weights = [jnp.exp2((g - new) * factor) for g in groups]
        top_ref[here, :] = new
        sum_ref[here, :] = sum_ref[here, :] * change + functools.reduce(jnp.add, weights)
        product = jnp.dot(
            jnp.concatenate([w.astype(BF16) for w in weights], axis=1),
            kv[pl.ds(start, count), pl.ds(HEAD_DIM, HEAD_DIM)],
            preferred_element_type=F32,
        )
        acc_ref[here, :] = acc_ref[here, :] * change + product

    def attend(r0, start, count, masked=False):
        chunk = 512
        if count <= chunk or count % chunk:
            one_step(r0, start, count, masked)
        else:
            def body(i, carry):
                one_step(r0, pl.multiple_of(start + i * chunk, chunk // 2), chunk, masked)
                return carry

            lax.fori_loop(0, count // chunk, body, 0)

    def class_start(b_, c_):
        return pl.multiple_of((c_ * 2 + b_) * part_keys, part_keys)

    for p in range(2, pairs):
        project(p)
    relay_a(kv_set)
    relay_a(row_set)
    for r in range(4):
        attend(r * block, class_start(b, c), part_keys)
    relay_b(kv_set)
    finish(kv_set, b)
    for r in range(4):
        attend(r * block, class_start(b, 1 - c), part_keys)
    relay_b(row_set)
    for r in range(4):
        attend(r * block, class_start(1 - b, c), part_keys)
    finish(row_set, b)
    finish(row_set, 1 - b)

    def place(s):
        v = link_at(s)
        safe = jnp.maximum(v, 0)
        owner = lax.div(safe, entities)

        def same(s2, total):
            w = link_at(s2)
            return total + jnp.where((w >= 0) & (lax.div(jnp.maximum(w, 0), entities) == owner), 1, 0)

        rank = jnp.int32(0)
        if slots <= 16:
            for s2 in range(s):
                rank = same(s2, rank)
        else:
            rank = lax.fori_loop(0, s, same, rank)
        rank = jnp.where(v >= 0, jnp.minimum(rank, MOST - 1), 0)
        seat = place_of(
            lax.div(owner, 4), lax.rem(lax.div(owner, 2), 2), lax.rem(owner, 2)
        )
        start = n * t + s * SUM_ROWS
        if not isinstance(s, int):
            start = pl.multiple_of(start, SUM_ROWS)
        kv[pl.ds(start, SUM_ROWS), pl.ds(0, HEAD_DIM)] = rows[seat, rank]
        kv[pl.ds(start, SUM_ROWS), pl.ds(HEAD_DIM, HEAD_DIM)] = rows[seat, MOST + rank]

    if slots <= 16:
        for s in range(slots):
            place(s)
    else:
        lax.fori_loop(0, slots, lambda s, carry: (place(s), carry)[1], 0)
    finish(kv_set, 1 - b)
    loads[5].wait()

    width = out_ref.shape[1]
    per_side = y_send.shape[0] // 2
    piece = width // per_side

    def y_copy(i):
        return pltpu.make_async_remote_copy(
            src_ref=y_send.at[i], dst_ref=y_recv.at[i],
            send_sem=y_send_sem.at[i], recv_sem=y_recv_sem.at[i],
            device_id=(me, 1 - hd), device_id_type=MESH,
        )

    for side in range(2):
        for r in range(2):
            r0 = (side * 2 + r) * block
            attend(r0, class_start(1 - b, 1 - c), part_keys)
            attend(r0, n * t, slots * SUM_ROWS, True)
            total = jnp.sum(sum_ref[pl.ds(r0, block), :], axis=1, keepdims=True)
            result = (acc_ref[pl.ds(r0, block), :] / total).astype(BF16)
            for i in range(heads // 2):
                h = r * (heads // 2) + i
                att[side, :, h * 128:(h + 1) * 128] = result[i * ht:(i + 1) * ht]
        for i in range(per_side):
            start = pl.multiple_of((1 - hd) * width + i * piece, piece)
            y_send[side * per_side + i] = jnp.dot(
                att[side], ow[:, pl.ds(start, piece)], preferred_element_type=F32
            ).astype(BF16)
            y_copy(side * per_side + i).start()
    both = jnp.concatenate([att[0], att[1]], axis=0)
    for i in range(per_side):
        start = pl.multiple_of(hd * width + i * piece, piece)
        part[:, i * piece:(i + 1) * piece] = jnp.dot(
            both, ow[:, pl.ds(start, piece)], preferred_element_type=F32
        )
    each(1, size, lambda k: link_a(a, lax.rem(a + k, size)).wait_send())
    link_b(b, 1 - b).wait_send()
    link_c(c, 1 - c).wait_send()
    sent(kv_set)
    sent(row_set)
    for side in range(2):
        for i in range(per_side):
            y_copy(side * per_side + i).wait_recv()
            here = (slice(side * ht, (side + 1) * ht), slice(i * piece, (i + 1) * piece))
            out_ref[here] = (part[here] + y_recv[side * per_side + i].astype(F32)).astype(BF16)
    for i in range(2 * per_side):
        y_copy(i).wait_send()


def shards(n, tokens, q_weight, k_weight, v_weight, out_weight, summary, links):
    t, d = tokens.shape
    local = q_weight.shape[1]
    heads = local // HEAD_DIM
    width = out_weight.shape[1] // 2
    entities = summary.shape[0]
    link_dev = links.shape[0]
    pieces = 2
    size = n // 4
    flat = summary.reshape(entities, SUM_ROWS * 2, HEAD_DIM)
    dma = pltpu.SemaphoreType.DMA
    hbm = pl.BlockSpec(memory_space=pl.ANY)
    return pl.pallas_call(
        functools.partial(kernel, n, entities, link_dev),
        out_shape=jax.ShapeDtypeStruct((t, width), BF16),
        in_specs=[hbm] * 6 + [pl.BlockSpec(memory_space=pltpu.SMEM)],
        out_specs=pl.BlockSpec(memory_space=pltpu.VMEM),
        scratch_shapes=[
            pltpu.VMEM((t, d), BF16),
            pltpu.VMEM((d, local), BF16),
            pltpu.VMEM((d, 2 * HEAD_DIM), BF16),
            pltpu.VMEM(out_weight.shape, BF16),
            pltpu.VMEM(flat.shape, BF16),
            pltpu.VMEM((heads * t, HEAD_DIM), BF16),
            pltpu.VMEM((n * t + n * link_dev * SUM_ROWS, 2 * HEAD_DIM), BF16),
            pltpu.VMEM((n, 2 * MOST, SUM_ROWS, HEAD_DIM), BF16),
            pltpu.VMEM((n, 1, 128), jnp.int32),
            pltpu.SMEM((n, 1, 128), jnp.int32),
            pltpu.VMEM((2, t // 2, local), BF16),
            pltpu.VMEM((t, width), F32),
            pltpu.VMEM((2 * pieces, t // 2, width // pieces), BF16),
            pltpu.VMEM((2 * pieces, t // 2, width // pieces), BF16),
            pltpu.VMEM((heads * t, HEAD_DIM), F32),
            pltpu.VMEM((heads * t, HEAD_DIM), F32),
            pltpu.VMEM((heads * t, HEAD_DIM), F32),
            dma((7,)), dma((n,)), dma((n,)), dma((size,)), dma((size,)), dma((2,)), dma((2,)),
            dma((size,)), dma((size,)), dma((2 * size,)),
            dma((size,)), dma((size,)), dma((2 * size,)),
            dma((2 * pieces,)), dma((2 * pieces,)),
        ],
        compiler_params=pltpu.CompilerParams(
            collective_id=0, has_side_effects=True, vmem_limit_bytes=56 * 1024 * 1024
        ),
    )(tokens, q_weight, k_weight, v_weight, out_weight, flat, links)


def solution(mesh):
    placed = (
        P("seq", None),
        P(None, "head"),
        P(None, "head"),
        P(None, "head"),
        P("head", None),
        P("seq", None, None, "head"),
        P("seq"),
    )
    return jax.shard_map(
        functools.partial(shards, mesh.shape["seq"]),
        mesh=mesh, in_specs=placed, out_specs=P("seq", "head"), check_vma=False,
    )
```

time: 41.1 us -> 36.4 us (0.89)
  the two profiles are of different devices: /device:TPU:9 before, /device:TPU:0 now
where the time goes in v2:
time: 36.4 us; the launch traced here: 36.2 us
  Pallas kernels  33.9 us (93%)
  local copies, waits for them, and re-layouts  1.67 us (5%)
  between operations  0.66 us (2%)
    pallas_call x1, Pallas kernels, shards(): pl.pallas_call(functools.partial(kernel, n, entities, link_dev), out_shap...  33.9 us
    unnamed x1, local copies, waits for them, and re-layouts  1.67 us

profile of v2, /device:TPU:0, one launch (start us, length us, event | category | flops | bytes accessed | tf_op | source)
XLA Modules:
  0.0 36.2 jit_solution(7901488697671707667)
XLA Ops:
  0.7 33.9 %shard_map.73 = bf16[128,1024]{1,0:T(8,128)(2,1)} custom-call(bf16[128,2048]{1,0:T(8,128)(2,1)} %tok_hbm.1, bf16[2048,1024]{1,0:T(8,128)(2,1)} %qw_hbm.1, bf16[2048,128]{1,0:T(8,128)(2,1)} %kw_hbm.1, bf16[2048,128]{1,0:T(8,128)(2,1)} %vw_hbm.1, bf16[1024,2048]{1,0:T(8,128)(2,1)} %ow_hbm.1, bf16[64,32,128]{2,1,0:T(8,128)(2,1)} %bitcast.1, s32[1]{0:T(128)S(6)} %copy.9.links_ref), custom_call_target="tpu_custom_call" | custom-call | tf_op jit(solution)/shard_map/pallas_call | solution.py:397
  34.5 1.7 %copy.10 = bf16[128,1024]{1,0:T(8,128)(2,1)} copy(bf16[128,1024]{1,0:T(8,128)(2,1)} %shard_map.73) | data formatting | bytes 524288

commit v3 on v2

--- a/solution.py
+++ b/solution.py
@@ -79,6 +79,7 @@
     each(1, size, lambda k: greet(ident(lax.rem(a + k, size), b, c), hd))
     greet(ident(a, 1 - b, c), hd)
     greet(ident(a, b, 1 - c), hd)
+    greet(ident(a, 1 - b, 1 - c), hd)
     greet(me, 1 - hd)
     for item in loads:
         item.start()
@@ -92,7 +93,7 @@
     sum_ref[...] = jnp.zeros(sum_ref.shape, F32)
     acc_ref[...] = jnp.zeros(acc_ref.shape, F32)
 
-    pl.semaphore_wait(barrier, size + 2)
+    pl.semaphore_wait(barrier, size + 3)
 
     def link_a(src_a, target_a):
         at = place_of(src_a, b, c)
@@ -102,21 +103,15 @@
             device_id=(ident(target_a, b, c), hd), device_id_type=MESH,
         )
 
-    def link_b(b_, target_b):
-        part_of = link_v.at[pl.ds((c * 2 + b_) * size, size)]
+    def link_bc(src_b, src_c, target_b, target_c, k):
+        part_of = link_v.at[pl.ds((src_c * 2 + src_b) * size, size)]
         return pltpu.make_async_remote_copy(
             src_ref=part_of, dst_ref=part_of,
-            send_sem=link_send_bc.at[0], recv_sem=link_recv_bc.at[0],
-            device_id=(ident(a, target_b, c), hd), device_id_type=MESH,
-        )
-
-    def link_c(c_, target_c):
-        part_of = link_v.at[pl.ds(c_ * 2 * size, 2 * size)]
-        return pltpu.make_async_remote_copy(
-            src_ref=part_of, dst_ref=part_of,
-            send_sem=link_send_bc.at[1], recv_sem=link_recv_bc.at[1],
-            device_id=(ident(a, b, target_c), hd), device_id_type=MESH,
-        )
+            send_sem=link_send_bc.at[k], recv_sem=link_recv_bc.at[k],
+            device_id=(ident(a, target_b, target_c), hd), device_id_type=MESH,
+        )
+
+    corners = ((1 - b, 1 - c), (1 - b, c), (b, 1 - c))
 
     each(1, size, lambda k: link_a(a, lax.rem(a + k, size)).start())
 
@@ -161,14 +156,14 @@
     def got(group, src):
         group[0](src, me, group[1].at[0]).wait_recv()
 
-    def relay_a(group):
+    def relay_a(group, low, high):
         def one(k):
             a_ = other(k)
             got(group, place_of(a_, b, c))
             to_b(*group, a_).start()
             to_c(*group, a_, b).start()
 
-        each(1, size, one)
+        each(low, high, one)
 
     def relay_b(group):
         def one(k):
@@ -199,13 +194,14 @@
 
     pairs = heads // 2
     each(1, size, lambda k: link_a(lax.rem(a + k, size), a).wait_recv())
-    link_b(b, 1 - b).start()
+    for k in range(3):
+        link_bc(b, c, *corners[k], k).start()
     loads[4].wait()
     project(0)
-    link_b(1 - b, b).wait_recv()
-    link_c(c, 1 - c).start()
     project(1)
-    link_c(1 - c, c).wait_recv()
+    relay_a(kv_set, 1, 2)
+    for k in range(3):
+        link_bc(*corners[k], b, c, k).wait_recv()
     to_scalar = pltpu.make_async_copy(link_v, link_s, load_sem.at[6])
     to_scalar.start()
     to_scalar.wait()
@@ -286,19 +282,22 @@
     def class_start(b_, c_):
         return pl.multiple_of((c_ * 2 + b_) * part_keys, part_keys)
 
+    relay_a(kv_set, 2, size)
     for p in range(2, pairs):
         project(p)
-    relay_a(kv_set)
-    relay_a(row_set)
     for r in range(4):
         attend(r * block, class_start(b, c), part_keys)
     relay_b(kv_set)
+    relay_a(row_set, 1, size)
     finish(kv_set, b)
     for r in range(4):
         attend(r * block, class_start(b, 1 - c), part_keys)
     relay_b(row_set)
     for r in range(4):
         attend(r * block, class_start(1 - b, c), part_keys)
+    finish(kv_set, 1 - b)
+    for r in range(4):
+        attend(r * block, class_start(1 - b, 1 - c), part_keys)
     finish(row_set, b)
     finish(row_set, 1 - b)
 
@@ -332,7 +331,6 @@
             place(s)
     else:
         lax.fori_loop(0, slots, lambda s, carry: (place(s), carry)[1], 0)
-    finish(kv_set, 1 - b)
     loads[5].wait()
 
     width = out_ref.shape[1]
@@ -349,7 +347,6 @@
     for side in range(2):
         for r in range(2):
             r0 = (side * 2 + r) * block
-            attend(r0, class_start(1 - b, 1 - c), part_keys)
             attend(r0, n * t, slots * SUM_ROWS, True)
             total = jnp.sum(sum_ref[pl.ds(r0, block), :], axis=1, keepdims=True)
             result = (acc_ref[pl.ds(r0, block), :] / total).astype(BF16)
@@ -369,8 +366,8 @@
             both, ow[:, pl.ds(start, piece)], preferred_element_type=F32
         )
     each(1, size, lambda k: link_a(a, lax.rem(a + k, size)).wait_send())
-    link_b(b, 1 - b).wait_send()
-    link_c(c, 1 - c).wait_send()
+    for k in range(3):
+        link_bc(b, c, *corners[k], k).wait_send()
     sent(kv_set)
     sent(row_set)
     for side in range(2):
@@ -417,7 +414,7 @@
             pltpu.VMEM((heads * t, HEAD_DIM), F32),
             pltpu.VMEM((heads * t, HEAD_DIM), F32),
             pltpu.VMEM((heads * t, HEAD_DIM), F32),
-            dma((7,)), dma((n,)), dma((n,)), dma((size,)), dma((size,)), dma((2,)), dma((2,)),
+            dma((7,)), dma((n,)), dma((n,)), dma((size,)), dma((size,)), dma((3,)), dma((3,)),
             dma((size,)), dma((size,)), dma((2 * size,)),
             dma((size,)), dma((size,)), dma((2 * size,)),
             dma((2 * pieces,)), dma((2 * pieces,)),

time: 36.4 us -> 34.1 us (0.937)
  Pallas kernels: 33.9 us -> 31.7 us
    pallas_call x1, Pallas kernels: 33.9 us -> 31.7 us  [shards(): pl.pallas_call(functools.partial(kernel, n, entities, link_dev), out_shap...]
where the time goes in v3:
time: 34.1 us; the launch traced here: 34 us
  Pallas kernels  31.7 us (93%)
  local copies, waits for them, and re-layouts  1.67 us (5%)
  between operations  0.66 us (2%)
    pallas_call x1, Pallas kernels, shards(): pl.pallas_call(functools.partial(kernel, n, entities, link_dev), out_shap...  31.7 us
    unnamed x1, local copies, waits for them, and re-layouts  1.67 us

profile of v3, /device:TPU:0, one launch (start us, length us, event | category | flops | bytes accessed | tf_op | source)
XLA Modules:
  0.0 34.0 jit_solution(3358251594782064054)
XLA Ops:
  0.7 31.7 %shard_map.73 = bf16[128,1024]{1,0:T(8,128)(2,1)} custom-call(bf16[128,2048]{1,0:T(8,128)(2,1)} %tok_hbm.1, bf16[2048,1024]{1,0:T(8,128)(2,1)} %qw_hbm.1, bf16[2048,128]{1,0:T(8,128)(2,1)} %kw_hbm.1, bf16[2048,128]{1,0:T(8,128)(2,1)} %vw_hbm.1, bf16[1024,2048]{1,0:T(8,128)(2,1)} %ow_hbm.1, bf16[64,32,128]{2,1,0:T(8,128)(2,1)} %bitcast.1, s32[1]{0:T(128)S(6)} %copy.9.links_ref), custom_call_target="tpu_custom_call" | custom-call | tf_op jit(solution)/shard_map/pallas_call | solution.py:394
  32.3 1.7 %copy.10 = bf16[128,1024]{1,0:T(8,128)(2,1)} copy(bf16[128,1024]{1,0:T(8,128)(2,1)} %shard_map.73) | data formatting | bytes 524288
